TPU v7x, 32 devices: a whole 2x2x4 slice. The times are simulated.
32 devices in a mesh: gz: 4 (over y, x), xy: 8 (over z, core).
Axes of the slice: x: 2, y: 2, z: 4, core: 2. Of those that a mesh axis runs over, the one named last changes fastest.
Arguments:
- velocity: float32 [3, 64, 256, 128], P(None, 'gz', 'xy'), may hold values from -6 to 6
- viscosity: float32 [64, 256, 128], P('gz', 'xy'), may hold values from 0.4 to 2
- frac: float32 [256, 3, 128], P(('gz', 'xy')), may hold values from 0 to 1
- force: float32 [256, 3, 128], P(('gz', 'xy')), may hold values from -24 to 24
- target: int32 [256, 1], P(('gz', 'xy')), may hold values from 0 to 7; in each aligned block of 8 rows (0 to 7, 8 to 15, ...) at most 2 rows name the same one
- z_offset: int32 [256], P(('gz', 'xy')), may hold values from -4 to 12
- y_offset: int32 [256], P(('gz', 'xy')), may hold values from -4 to 28
Outputs:
- new_velocity: float32 [3, 64, 256, 128], P(None, 'gz', 'xy')
- point_velocity: float32 [256, 3, 128], P(('gz', 'xy'))
Inputs may be any that keep to these rules, and one draw needn't show every extreme that they name: Among the 8 blocks stored on one device, no value of target occurs more than 2 times, and some device's blocks hold one value exactly 2 times.
All inputs are finite; a program needn't handle non-finite values.
Results may differ from a plain program's by a relative error of at most 0.0003.
Values sent between devices are 32-bit elements; how exact they have to be, the bound alone decides.
A program may use at most 64 MiB of HBM per device.

v0:
```python
import functools

import jax
import jax.numpy as jnp
from jax import lax
from jax.experimental import pallas as pl
from jax.experimental.pallas import tpu as pltpu
from jax.sharding import PartitionSpec as P

BOX = 8
CAP = 2
FAR = 4096.0
ZP = 7
YP = 8
GROUP = 8
TOGETHER = 4
MESH = pl.DeviceIdType.MESH
VMEM_LIMIT = 63 * 1024 * 1024


def peers(gz, xy, rows, columns):
    def each(body):
        for dr in (-1, 0, 1):
            inside = jnp.logical_and(gz + dr >= 0, gz + dr < rows)

            @pl.when(inside)
            def _(dr=dr):
                for k in range(1 if dr == 0 else 0, columns):
                    column = xy + k
                    body(dr, jnp.where(column >= columns, column - columns, column))

    return each


def each_row(gz, rows, body):
    for dr in (-1, 0, 1):
        inside = jnp.logical_and(gz + dr >= 0, gz + dr < rows)
        pl.when(inside)(functools.partial(body, dr))


def greet(gz, xy, rows, columns):
    barrier = pltpu.get_barrier_semaphore()

    def signal(dr, column):
        pl.semaphore_signal(barrier, inc=1, device_id=(gz + dr, column), device_id_type=MESH)

    peers(gz, xy, rows, columns)(signal)
    near = (
        1 + (gz > 0).astype(jnp.int32) + (gz < rows - 1).astype(jnp.int32)
    )
    return lambda: pl.semaphore_wait(barrier, near * columns - 1)


def matches(target_ref, count, column):
    first, second = jnp.int32(-1), jnp.int32(-1)
    for j in range(count):
        hit = target_ref[j] == column
        second = jnp.where(jnp.logical_and(hit, jnp.logical_and(first >= 0, second < 0)), j, second)
        first = jnp.where(jnp.logical_and(hit, first < 0), j, first)
    return first, second


def laplace(centre, visc, z_low, z_high, y_low, y_high, coeffs, lane):
    length = centre.shape[-1]
    x_high = jnp.where(lane == length - 1, 0.0, pltpu.roll(centre, length - 1, 1))
    x_low = jnp.where(lane == 0, 0.0, pltpu.roll(centre, 1, 1))
    total = coeffs[0] * (z_high - centre) + coeffs[1] * (z_low - centre)
    total = total + coeffs[2] * (y_high - centre) + coeffs[3] * (y_low - centre)
    total = total + coeffs[4] * (x_high - centre) + coeffs[5] * (x_low - centre)
    return centre + 0.08 * total


def x_coeffs(visc, lane):
    length = visc.shape[-1]
    high = jnp.where(lane == length - 1, 0.0, pltpu.roll(visc, length - 1, 1))
    low = jnp.where(lane == 0, 0.0, pltpu.roll(visc, 1, 1))
    return 0.5 * (visc + high), 0.5 * (visc + low)


def exchange_kernel(
    rows, columns, target_ref, zoff_ref, yoff_ref, velocity_ref, viscosity_ref, frac_ref, force_ref,
    moved_ref, slots_ref, meta_ref,
    pad, once, staging, layers_out, layers_in, corner_out, corner_in,
    load_sem, ab_send, ab_recv, halo_send, halo_recv, corner_send, corner_recv, c_send, c_recv,
):
    gz, xy = lax.axis_index("gz"), lax.axis_index("xy")
    depth, breadth = velocity_ref.shape[1], velocity_ref.shape[2]
    length = velocity_ref.shape[3]
    wait_greeting = greet(gz, xy, rows, columns)
    loads = (
        pltpu.make_async_copy(
            velocity_ref, pad.at[0:3, 2 : 2 + depth, 8 : 8 + breadth], load_sem.at[0]
        ),
        pltpu.make_async_copy(
            viscosity_ref, pad.at[3, 2 : 2 + depth, 8 : 8 + breadth], load_sem.at[1]
        ),
    )
    for load in loads:
        load.start()

    lanes = lax.broadcasted_iota(jnp.int32, (1, length), 1)
    count = frac_ref.shape[1]

    def stage(column, unused):
        for rank, block in enumerate(matches(target_ref, count, column)):
            at = jnp.maximum(block, 0)
            there = block >= 0
            z = jnp.where(there, zoff_ref[at].astype(jnp.float32), FAR)
            y = jnp.where(there, yoff_ref[at].astype(jnp.float32), FAR)
            staging[column, rank, 0:3, :] = frac_ref[:, at, :]
            staging[column, rank, 3:6, :] = force_ref[:, at, :]
            staging[column, rank, 6:7, :] = jnp.where(lanes == 0, z, y)
            staging[column, rank, 7:8, :] = jnp.zeros((1, length), jnp.float32)
        return unused

    lax.fori_loop(0, columns, stage, 0)
    each_peer = peers(gz, xy, rows, columns)

    def block_copy(dr, column):
        return pltpu.make_async_remote_copy(
            src_ref=staging.at[column],
            dst_ref=slots_ref.at[0, 1 - dr, xy],
            send_sem=ab_send.at[dr + 1],
            recv_sem=ab_recv.at[1 - dr],
            device_id=(gz + dr, column),
            device_id_type=MESH,
        )

    def whole_row(dr):
        span = pl.ds(0, columns - (1 if dr == 0 else 0))
        return pltpu.make_async_remote_copy(
            src_ref=staging.at[span],
            dst_ref=slots_ref.at[0, dr + 1, span],
            send_sem=ab_send.at[dr + 1],
            recv_sem=ab_recv.at[dr + 1],
            device_id=(gz, xy),
            device_id_type=MESH,
        )

    wait_greeting()
    each_peer(lambda dr, column: block_copy(dr, column).start())
    slots_ref[0, 1, xy] = staging[xy]

    has = (gz > 0, gz < rows - 1, xy > 0, xy < columns - 1)
    device = ((gz - 1, xy), (gz + 1, xy), (gz, xy - 1), (gz, xy + 1))
    own_y = slice(8, 8 + breadth)
    own_z = slice(2, 2 + depth)

    def halo_copies(side):
        if side == 0:
            cut, land = slice(0, 2), (slice(2 + depth, 4 + depth), own_y)
        elif side == 1:
            cut, land = slice(depth - 2, depth), (slice(0, 2), own_y)
        if side < 2:
            sources = (velocity_ref.at[:, cut], viscosity_ref.at[cut])
            lands = (pad.at[(slice(0, 3),) + land], pad.at[(3,) + land])
        else:
            sources, lands = (layers_out.at[side - 2],), (layers_in.at[3 - side],)
        return [
            pltpu.make_async_remote_copy(
                src_ref=source,
                dst_ref=spot,
                send_sem=halo_send.at[side, number],
                recv_sem=halo_recv.at[side, number],
                device_id=device[side],
                device_id_type=MESH,
            )
            for number, (source, spot) in enumerate(zip(sources, lands))
        ]

    def on_side(side, action):
        @pl.when(has[side])
        def _():
            for copy in halo_copies(side):
                action(copy)

    for side in (0, 1):
        on_side(side, lambda copy: copy.start())

    zeros_z = jnp.zeros((4, 2, breadth, length), jnp.float32)
    zeros_y = jnp.zeros((4, depth, 8, length), jnp.float32)

    @pl.when(gz == 0)
    def _():
        pad[:, 0:2, 8 : 8 + breadth, :] = zeros_z
        slots_ref[0, 0] = jnp.full(slots_ref.shape[2:], FAR, jnp.float32)

    @pl.when(gz == rows - 1)
    def _():
        pad[:, 2 + depth : 4 + depth, 8 : 8 + breadth, :] = zeros_z
        slots_ref[0, 2] = jnp.full(slots_ref.shape[2:], FAR, jnp.float32)

    @pl.when(xy == 0)
    def _():
        pad[:, 2 : 2 + depth, 0:8, :] = zeros_y
        slots_ref[1] = jnp.full(slots_ref.shape[1:], FAR, jnp.float32)

    @pl.when(xy == columns - 1)
    def _():
        pad[:, 2 : 2 + depth, 8 + breadth : 16 + breadth, :] = zeros_y
        slots_ref[2] = jnp.full(slots_ref.shape[1:], FAR, jnp.float32)

    for load in loads:
        load.wait()
    for side, start in ((2, 8), (3, 6 + breadth)):
        for part in range(4):
            for layer in range(2):
                layers_out[side - 2, part, layer * depth : (layer + 1) * depth, :] = pad[
                    part, 2 : 2 + depth, start + layer, :
                ]
        on_side(side, lambda copy: copy.start())

    corners = []
    for number, (dz, dy) in enumerate(((-1, -1), (-1, 1), (1, -1), (1, 1))):
        z_in = 2 if dz < 0 else 1 + depth
        y_in = 8 if dy < 0 else 7 + breadth
        z_out = 1 if dz < 0 else 2 + depth
        y_out = 7 if dy < 0 else 8 + breadth
        present = jnp.logical_and(has[0 if dz < 0 else 1], has[2 if dy < 0 else 3])
        for part in range(4):
            corner_out[number, part : part + 1, :] = pad[part, z_in, y_in : y_in + 1, :]
        copy = pltpu.make_async_remote_copy(
            src_ref=corner_out.at[number],
            dst_ref=corner_in.at[3 - number],
            send_sem=corner_send.at[number],
            recv_sem=corner_recv.at[3 - number],
            device_id=(gz + dz, xy + dy),
            device_id_type=MESH,
        )
        arrival = pltpu.make_async_remote_copy(
            src_ref=corner_out.at[number],
            dst_ref=corner_in.at[number],
            send_sem=corner_send.at[number],
            recv_sem=corner_recv.at[number],
            device_id=(gz + dz, xy + dy),
            device_id_type=MESH,
        )
        corners.append((present, copy, arrival, number, z_out, y_out))
    for present, copy, arrival, number, z_out, y_out in corners:
        pl.when(present)(lambda copy=copy: copy.start())

    lane = lax.broadcasted_iota(jnp.int32, (breadth + 16, length), 1)
    line = lax.broadcasted_iota(jnp.int32, (breadth + 16, length), 0)
    low_y = jnp.where(xy > 0, 0, 8)
    high_y = jnp.where(xy < columns - 1, breadth + 16, breadth + 8)
    in_grid = jnp.logical_and(line >= low_y, line < high_y)
    first_z = jnp.where(gz > 0, 0, 2)
    last_z = jnp.where(gz < rows - 1, depth + 3, depth + 1)

    def first_sweep(z):
        visc = pad[3, z]
        size = visc.shape[0]
        cx_high, cx_low = x_coeffs(visc, lane)
        coeffs = (
            0.5 * (visc + pad[3, z + 1]),
            0.5 * (visc + pad[3, z - 1]),
            0.5 * (visc + pltpu.roll(visc, size - 1, 0)),
            0.5 * (visc + pltpu.roll(visc, 1, 0)),
            cx_high,
            cx_low,
        )
        z_inside = jnp.logical_and(z >= first_z, z <= last_z)
        keep = jnp.logical_and(in_grid, z_inside)
        for part in range(3):
            centre = pad[part, z]
            new = laplace(
                centre, visc, pad[part, z - 1], pad[part, z + 1],
                pltpu.roll(centre, 1, 0), pltpu.roll(centre, size - 1, 0), coeffs, lane,
            )
            once[part, z - 1] = jnp.where(keep, new, 0.0)

    own_lane = lane[:breadth]

    def second_sweep(z):
        visc = pad[3, z, 8 : 8 + breadth, :]
        cx_high, cx_low = x_coeffs(visc, own_lane)
        coeffs = (
            0.5 * (visc + pad[3, z + 1, 8 : 8 + breadth, :]),
            0.5 * (visc + pad[3, z - 1, 8 : 8 + breadth, :]),
            0.5 * (visc + pad[3, z, 9 : 9 + breadth, :]),
            0.5 * (visc + pad[3, z, 7 : 7 + breadth, :]),
            cx_high,
            cx_low,
        )
        for part in range(3):
            moved_ref[part, z - 2] = laplace(
                once[part, z - 1, 8 : 8 + breadth, :], visc,
                once[part, z - 2, 8 : 8 + breadth, :], once[part, z, 8 : 8 + breadth, :],
                once[part, z - 1, 7 : 7 + breadth, :], once[part, z - 1, 9 : 9 + breadth, :],
                coeffs, own_lane,
            )

    def loop(low, high, body):
        def step(z, unused):
            body(z)
            return unused

        lax.fori_loop(low, high, step, 0)

    arrives = ((1, 0), (0, 1), (3, 2), (2, 3))

    def wait_side(side, neighbour):
        @pl.when(has[neighbour])
        def _():
            for copy in halo_copies(side):
                copy.wait_recv()
            if side >= 2:
                start = 6 if side == 3 else 8 + breadth
                for part in range(4):
                    for layer in range(2):
                        pad[part, 2 : 2 + depth, start + layer, :] = layers_in[
                            3 - side, part, layer * depth : (layer + 1) * depth, :
                        ]

    forwards = []
    for number, (there, column, side) in enumerate(((has[3], xy + 1, 1), (has[2], xy - 1, 2))):
        for dr in (-1, 0, 1):
            copy = pltpu.make_async_remote_copy(
                src_ref=slots_ref.at[0, dr + 1],
                dst_ref=slots_ref.at[side, dr + 1],
                send_sem=c_send.at[number, dr + 1],
                recv_sem=c_recv.at[number, dr + 1],
                device_id=(gz, column),
                device_id_type=MESH,
            )
            forwards.append((there, copy, dr, has[2 + number]))

    def forward(row):
        for there, copy, dr, unused in forwards:
            if dr == row:
                pl.when(there)(lambda copy=copy: copy.start())

    whole_row(0).wait_recv()
    forward(0)
    wait_side(2, 3)
    wait_side(3, 2)
    loop(3, 3 + depth // 4, first_sweep)
    for dr in (-1, 1):
        pl.when(has[0 if dr < 0 else 1])(lambda dr=dr: whole_row(dr).wait_recv())
        forward(dr)
    loop(3 + depth // 4, 1 + depth, first_sweep)

    wait_side(0, 1)
    wait_side(1, 0)
    for present, copy, arrival, number, z_out, y_out in corners:

        @pl.when(present)
        def _(arrival=arrival, number=number, z_out=z_out, y_out=y_out):
            arrival.wait_recv()
            for part in range(4):
                pad[part, z_out, y_out : y_out + 1, :] = corner_in[number, part : part + 1, :]

        @pl.when(jnp.logical_not(present))
        def _(z_out=z_out, y_out=y_out):
            for part in range(4):
                pad[part, z_out, y_out : y_out + 1, :] = jnp.zeros((1, length), jnp.float32)

    for z in (1, 2, 1 + depth, 2 + depth):
        first_sweep(z)
    loop(2, 2 + depth, second_sweep)

    for unused, copy, dr, comes in forwards:
        pl.when(comes)(lambda copy=copy: copy.wait_recv())
    for side in range(3):
        for dr in range(3):
            shift = jnp.where(lanes == 0, (dr - 1) * depth, (0, -breadth, breadth)[side])
            for column in range(columns):
                at = ((side * 3 + dr) * columns + column) * CAP
                for rank in range(CAP):
                    row = slots_ref[side, dr, column, rank, 6:7, :].astype(jnp.int32)
                    meta_ref[at + rank : at + rank + 1, :] = row + shift

    each_row(gz, rows, lambda dr: whole_row(dr).wait_send())
    for side in range(4):
        on_side(side, lambda copy: copy.wait_send())
    for present, copy, arrival, number, z_out, y_out in corners:
        pl.when(present)(lambda copy=copy: copy.wait_send())
    for there, copy, unused, comes in forwards:
        pl.when(there)(lambda copy=copy: copy.wait_send())


def phi(radius):
    x2 = radius * radius * 0.6168502750680849
    c = 1.0 / 479001600.0
    for factor in (-1.0 / 3628800.0, 1.0 / 40320.0, -1.0 / 720.0, 1.0 / 24.0, -0.5, 1.0):
        c = c * x2 + factor
    return jnp.where(jnp.abs(radius) < 2.0, 0.5 * c * c, 0.0)


def split(value):
    high = value.astype(jnp.bfloat16)
    return high, (value - high.astype(jnp.float32)).astype(jnp.bfloat16)


def product(left, right, contract):
    dims = (((1,), (contract,)), ((), ()))
    dot = functools.partial(
        lax.dot_general, dimension_numbers=dims, preferred_element_type=jnp.float32
    )
    (left_high, left_low), (right_high, right_low) = left, right
    return dot(left_high, right_high) + dot(left_high, right_low) + dot(left_low, right_high)


def points_kernel(
    columns, meta_ref, slots_ref, moved_ref, new_ref, partial_ref, field, wx_high, wx_low, listed, load_sem, store_sem
):
    depth, breadth, length = moved_ref.shape[1:]
    inner = field.at[:, ZP : ZP + depth, YP : YP + breadth]
    load = pltpu.make_async_copy(moved_ref, inner, load_sem)
    load.start()
    total_z = field.shape[1]
    field[:, 0:ZP] = jnp.zeros((3, ZP) + field.shape[2:], jnp.float32)
    field[:, ZP + depth :] = jnp.zeros((3, total_z - ZP - depth) + field.shape[2:], jnp.float32)
    field[:, ZP : ZP + depth, 0:YP] = jnp.zeros((3, depth, YP, length), jnp.float32)
    field[:, ZP : ZP + depth, YP + breadth :] = jnp.zeros(
        (3, depth, field.shape[2] - YP - breadth, length), jnp.float32
    )
    partial_ref[...] = jnp.zeros_like(partial_ref)
    slot_count = meta_ref.shape[0]

    def list_some(group, found):
        for number in range(GROUP):
            slot = group * GROUP + number
            z, y = meta_ref[slot, 0], meta_ref[slot, 1]
            meets = (z > -BOX) & (z < depth) & (y > -BOX) & (y < breadth)
            listed[found] = slot
            found = found + meets.astype(jnp.int32)
        return found

    found = lax.fori_loop(0, slot_count // GROUP, list_some, jnp.int32(0))
    rounds = (found + TOGETHER - 1) // TOGETHER
    load.wait()

    line = lax.broadcasted_iota(jnp.int32, (BOX, length), 0)
    rel = line.astype(jnp.float32)
    far = lax.broadcasted_iota(jnp.int32, (length, length), 0).astype(jnp.float32)

    def members(number):
        for other in range(TOGETHER):
            at = number * TOGETHER + other
            slot = listed[jnp.minimum(at, found - 1)]
            yield at, at < found, slot, meta_ref[slot, 0], meta_ref[slot, 1]

    def near_weights(tile, z, y):
        wz = phi(2.0 + (BOX - 5) * tile[0:1] - rel)
        wy = phi(2.0 + (BOX - 5) * tile[1:2] - rel)
        wz = jnp.where((z + line >= 0) & (z + line < depth), wz, 0.0)
        wy = jnp.where((y + line >= 0) & (y + line < breadth), wy, 0.0)
        return wz, wy

    def box_of(z, y):
        return (slice(None), pl.ds(z + ZP, BOX), pl.ds(y + YP, BOX), slice(None))

    def spread(number, unused):
        adds = []
        for at, counts, slot, z, y in members(number):
            tile = slots_ref[slot]
            wz, wy = near_weights(tile, z, y)
            wy = jnp.where(counts, wy, 0.0)
            wx = split(phi(2.0 + (length - 5) * tile[2:3] - far))
            wx_high[at], wx_low[at] = wx
            pulled = tile[3:6][:, None, :] * wz[None]
            coeff = pulled[:, :, None, :] * wy[None, None]
            boxes = product(split(coeff.reshape(3 * BOX * BOX, length)), wx, 1)
            adds.append((box_of(z, y), boxes.reshape(3, BOX, BOX, length)))
        for box, boxes in adds:
            field[box] = field[box] + boxes
        return unused

    lax.fori_loop(0, rounds, spread, 0)
    store = pltpu.make_async_copy(inner, new_ref, store_sem)
    store.start()

    def sample(number, unused):
        results = []
        for at, counts, slot, z, y in members(number):
            wz, wy = near_weights(slots_ref[slot], z, y)
            cells = field[box_of(z, y)].reshape(3 * BOX * BOX, length)
            taken = product(split(cells), (wx_high[at], wx_low[at]), 0)
            taken = taken.reshape(3, BOX, BOX, length)
            summed = jnp.sum(taken * wz[None, :, None, :], axis=1)
            results.append((slot, jnp.sum(summed * wy[None], axis=1)))
        for slot, values in results:
            partial_ref[slot // CAP, pl.ds(3 * lax.rem(slot, CAP), 3), :] = values
        return unused

    lax.fori_loop(0, rounds, sample, 0)
    store.wait()


def return_kernel(
    rows, columns, target_ref, partial_ref, out_ref,
    side_in, summed, gathered, c_send, c_recv, ab_send, ab_recv,
):
    gz, xy = lax.axis_index("gz"), lax.axis_index("xy")
    wait_greeting = greet(gz, xy, rows, columns)
    wait_greeting()
    has_low, has_high = xy > 0, xy < columns - 1
    copies = []
    for number, (there, column) in enumerate(((has_low, xy - 1), (has_high, xy + 1))):
        copy = pltpu.make_async_remote_copy(
            src_ref=partial_ref.at[number + 1],
            dst_ref=side_in.at[1 - number],
            send_sem=c_send.at[number],
            recv_sem=c_recv.at[1 - number],
            device_id=(gz, column),
            device_id_type=MESH,
        )
        arrival = pltpu.make_async_remote_copy(
            src_ref=partial_ref.at[number + 1],
            dst_ref=side_in.at[number],
            send_sem=c_send.at[number],
            recv_sem=c_recv.at[number],
            device_id=(gz, column),
            device_id_type=MESH,
        )
        copies.append((there, copy))
        pl.when(there)(lambda copy=copy: copy.start())

        @pl.when(jnp.logical_not(there))
        def _(number=number):
            side_in[number] = jnp.zeros(side_in.shape[1:], jnp.float32)

        copies[-1] = (there, copy, arrival)
    for there, copy, arrival in copies:
        pl.when(there)(lambda arrival=arrival: arrival.wait_recv())
    summed[...] = partial_ref[0] + side_in[0] + side_in[1]

    each_peer = peers(gz, xy, rows, columns)

    def block_copy(dr, column):
        return pltpu.make_async_remote_copy(
            src_ref=summed.at[dr + 1, column],
            dst_ref=gathered.at[1 - dr, xy],
            send_sem=ab_send.at[dr + 1],
            recv_sem=ab_recv.at[1 - dr],
            device_id=(gz + dr, column),
            device_id_type=MESH,
        )

    def whole_row(dr):
        span = pl.ds(0, columns - (1 if dr == 0 else 0))
        return pltpu.make_async_remote_copy(
            src_ref=summed.at[dr + 1, span],
            dst_ref=gathered.at[dr + 1, span],
            send_sem=ab_send.at[dr + 1],
            recv_sem=ab_recv.at[dr + 1],
            device_id=(gz, xy),
            device_id_type=MESH,
        )

    each_peer(lambda dr, column: block_copy(dr, column).start())
    gathered[1, xy] = summed[1, xy]

    @pl.when(gz == 0)
    def _():
        gathered[0] = jnp.zeros(gathered.shape[1:], jnp.float32)

    @pl.when(gz == rows - 1)
    def _():
        gathered[2] = jnp.zeros(gathered.shape[1:], jnp.float32)

    each_row(gz, rows, lambda dr: whole_row(dr).wait_recv())
    count = out_ref.shape[1]
    for j in range(count):
        column = target_ref[j]
        rank = jnp.int32(0)
        for earlier in range(j):
            rank = rank + (target_ref[earlier] == column).astype(jnp.int32)
        tile = gathered[0, column] + gathered[1, column] + gathered[2, column]
        out_ref[:, j, :] = jnp.where(rank == 0, tile[0:3], tile[3:6])
    each_row(gz, rows, lambda dr: whole_row(dr).wait_send())
    for there, copy, arrival in copies:
        pl.when(there)(lambda copy=copy: copy.wait_send())


def shards(rows, columns, velocity, viscosity, frac, force, target, z_offset, y_offset):
    parts, depth, breadth, length = velocity.shape
    target = target.reshape(target.shape[0])
    frac, force = jnp.transpose(frac, (1, 0, 2)), jnp.transpose(force, (1, 0, 2))
    f32 = jnp.float32
    vmem = pl.BlockSpec(memory_space=pltpu.VMEM)
    smem = pl.BlockSpec(memory_space=pltpu.SMEM)
    hbm = pl.BlockSpec(memory_space=pltpu.HBM)
    anyw = pl.BlockSpec(memory_space=pl.ANY)
    dma = pltpu.SemaphoreType.DMA
    slot_count = 9 * columns * CAP
    moved, slots, meta = pl.pallas_call(
        functools.partial(exchange_kernel, rows, columns),
        out_shape=(
            jax.ShapeDtypeStruct(velocity.shape, f32),
            jax.ShapeDtypeStruct((3, 3, columns, CAP, 8, length), f32),
            jax.ShapeDtypeStruct((slot_count, length), jnp.int32),
        ),
        in_specs=[smem, smem, smem, hbm, hbm, vmem, vmem],
        out_specs=(vmem, vmem, vmem),
        scratch_shapes=[
            pltpu.VMEM((4, depth + 4, breadth + 16, length), f32),
            pltpu.VMEM((3, depth + 2, breadth + 16, length), f32),
            pltpu.VMEM((columns, CAP, 8, length), f32),
            pltpu.VMEM((2, 4, 2 * depth, length), f32),
            pltpu.VMEM((2, 4, 2 * depth, length), f32),
            pltpu.VMEM((4, 8, length), f32),
            pltpu.VMEM((4, 8, length), f32),
            dma((2,)), dma((3,)), dma((3,)), dma((4, 2)), dma((4, 2)),
            dma((4,)), dma((4,)), dma((2, 3)), dma((2, 3)),
        ],
        compiler_params=pltpu.CompilerParams(
            collective_id=0, has_side_effects=True, vmem_limit_bytes=VMEM_LIMIT
        ),
    )(target, z_offset, y_offset, velocity, viscosity, frac, force)

    new_velocity, partial = pl.pallas_call(
        functools.partial(points_kernel, columns),
        out_shape=(
            jax.ShapeDtypeStruct(velocity.shape, f32),
            jax.ShapeDtypeStruct((slot_count // CAP, 8, length), f32),
        ),
        in_specs=[smem, vmem, anyw],
        out_specs=(anyw, vmem),
        scratch_shapes=[
            pltpu.VMEM((3, depth + 2 * ZP, breadth + 2 * YP, length), f32),
            pltpu.VMEM((slot_count + TOGETHER, length, length), jnp.bfloat16),
            pltpu.VMEM((slot_count + TOGETHER, length, length), jnp.bfloat16),
            pltpu.SMEM((slot_count + 1,), jnp.int32),
            dma(()), dma(()),
        ],
        compiler_params=pltpu.CompilerParams(vmem_limit_bytes=VMEM_LIMIT),
    )(meta, slots.reshape(slot_count, 8, length), moved)

    point_velocity = pl.pallas_call(
        functools.partial(return_kernel, rows, columns),
        out_shape=jax.ShapeDtypeStruct(frac.shape, f32),
        in_specs=[smem, vmem],
        out_specs=vmem,
        scratch_shapes=[
            pltpu.VMEM((2, 3, columns, 8, length), f32),
            pltpu.VMEM((3, columns, 8, length), f32),
            pltpu.VMEM((3, columns, 8, length), f32),
            dma((2,)), dma((2,)), dma((3,)), dma((3,)),
        ],
        compiler_params=pltpu.CompilerParams(
            collective_id=1, has_side_effects=True, vmem_limit_bytes=VMEM_LIMIT
        ),
    )(target, partial.reshape(3, 3, columns, 8, length))
    return new_velocity, jnp.transpose(point_velocity, (1, 0, 2))


def solution(mesh):
    placed = (
        P(None, "gz", "xy", None),
        P("gz", "xy", None),
        P(("gz", "xy"), None, None),
        P(("gz", "xy"), None, None),
        P(("gz", "xy"), None),
        P(("gz", "xy")),
        P(("gz", "xy")),
    )
    return jax.shard_map(
        functools.partial(shards, mesh.shape["gz"], mesh.shape["xy"]),
        mesh=mesh,
        in_specs=placed,
        out_specs=(P(None, "gz", "xy", None), P(("gz", "xy"), None, None)),
        check_vma=False,
    )
```

profile of v0, /device:TPU:0, one launch (start us, length us, event | category | flops | bytes accessed | tf_op | source)
XLA Modules:
  0.0 43.9 jit_solution(6582490472712834119)
XLA Ops:
  0.6 21.6 %shard_map.86 = (f32[3,16,32,128]{3,2,1,0:T(8,128)}, f32[3,3,8,2,8,128]{5,4,3,2,1,0:T(8,128)}, s32[144,128]{1,0:T(8,128)}) custom-call(s32[8]{0:T(128)} %bitcast.11, s32[8]{0:T(128)} %zoff_ref.1, s32[8]{0:T(128)} %yoff_ref.1, f32[3,16,32,128]{3,2,1,0:T(8,128)} %velocity_ref.1, f32[16,32,128]{2,1,0:T(8,128)} %viscosity_ref.1, f32[3,8,128]{2,1,0:T(8,128)} %bitcast.9, ...), custom_call_target="tpu_custom_call" | custom-call | tf_op jit(solution)/shard_map/pallas_call | solution.py:588
  22.2 7.4 %shard_map.87 = (f32[3,16,32,128]{3,2,1,0:T(8,128)}, f32[72,8,128]{2,1,0:T(8,128)}) custom-call(s32[144,128]{1,0:T(8,128)} %get-tuple-element.7.meta_ref, f32[144,8,128]{2,1,0:T(8,128)} %bitcast.6, f32[3,16,32,128]{3,2,1,0:T(8,128)} %get-tuple-element.9.moved_ref), custom_call_target="tpu_custom_call" | custom-call | tf_op jit(solution)/shard_map/pallas_call | solution.py:613
  29.7 12.9 %shard_map.88 = f32[3,8,128]{2,1,0:T(8,128)} custom-call(s32[8]{0:T(128)} %bitcast.12, f32[3,3,8,8,128]{4,3,2,1,0:T(8,128)} %bitcast.7), custom_call_target="tpu_custom_call" | custom-call | tf_op jit(solution)/shard_map/pallas_call | solution.py:631
  42.6 1.3 %copy.10 = f32[8,3,128]{2,0,1:T(8,128)} copy(f32[8,3,128]{2,0,1:T(8,128)} %bitcast.8) | data formatting | bytes 24576
where the time goes:
time: 44.4 us; the launch traced here: 43.9 us
  Pallas kernels  41.9 us (94%)
  local copies, waits for them, and re-layouts  1.31 us (3%)
  between operations  0.66 us (1%)
    pallas_call x1, Pallas kernels, shards(): pl.pallas_call(functools.partial(exchange_kernel, rows, columns), out_sha...  21.6 us
    pallas_call x1, Pallas kernels, shards(): pl.pallas_call(functools.partial(return_kernel, rows, columns), out_shape...  12.9 us
    pallas_call x1, Pallas kernels, shards(): pl.pallas_call(functools.partial(points_kernel, columns), out_shape=(jax....  7.45 us
    unnamed x1, local copies, waits for them, and re-layouts  1.31 us

commit v1 on v0

--- a/solution.py
+++ b/solution.py
@@ -15,7 +15,7 @@
 GROUP = 8
 TOGETHER = 4
 MESH = pl.DeviceIdType.MESH
-VMEM_LIMIT = 63 * 1024 * 1024
+VMEM_LIMIT = 24 * 1024 * 1024
 
 
 def peers(gz, xy, rows, columns):
@@ -578,6 +578,9 @@
     parts, depth, breadth, length = velocity.shape
     target = target.reshape(target.shape[0])
     frac, force = jnp.transpose(frac, (1, 0, 2)), jnp.transpose(force, (1, 0, 2))
+    held = lambda array: pltpu.with_memory_space_constraint(array, pltpu.HBM)
+    velocity, viscosity, frac, force = held(velocity), held(viscosity), held(frac), held(force)
+    target, z_offset, y_offset = held(target), held(z_offset), held(y_offset)
     f32 = jnp.float32
     vmem = pl.BlockSpec(memory_space=pltpu.VMEM)
     smem = pl.BlockSpec(memory_space=pltpu.SMEM)

time: 44.4 us -> 41 us (0.923); the launches traced: 43.9 us -> 41.4 us
  Pallas kernels: 41.9 us -> 40.1 us
  local copies, waits for them, and re-layouts: 1.31 us -> 0.6 us
    pallas_call x1, Pallas kernels: 7.45 us -> 4.79 us  [shards(): pl.pallas_call(functools.partial(points_kernel, columns), out_shape=(jax....]
    pallas_call x1, Pallas kernels: 12.9 us -> 14.9 us  [shards(): pl.pallas_call(functools.partial(return_kernel, rows, columns), out_shape...]
    pallas_call x1, Pallas kernels: 21.6 us -> 20.5 us  [shards(): pl.pallas_call(functools.partial(exchange_kernel, rows, columns), out_sha...]
    unnamed x1, local copies, waits for them, and re-layouts: 1.31 us -> 0.6 us
where the time goes in v1:
time: 41 us; the launch traced here: 41.4 us
  Pallas kernels  40.1 us (98%)
  between operations  0.66 us (2%)
  local copies, waits for them, and re-layouts  0.6 us (1%)
    pallas_call x1, Pallas kernels, shards(): pl.pallas_call(functools.partial(exchange_kernel, rows, columns), out_sha...  20.5 us
    pallas_call x1, Pallas kernels, shards(): pl.pallas_call(functools.partial(return_kernel, rows, columns), out_shape...  14.9 us
    pallas_call x1, Pallas kernels, shards(): pl.pallas_call(functools.partial(points_kernel, columns), out_shape=(jax....  4.79 us

profile of v1, /device:TPU:0, one launch (start us, length us, event | category | flops | bytes accessed | tf_op | source)
XLA Modules:
  0.0 41.4 jit_solution(5833273538108946215)
XLA Ops:
  0.6 20.5 %shard_map.86 = (f32[3,16,32,128]{3,2,1,0:T(8,128)S(1)}, f32[3,3,8,2,8,128]{5,4,3,2,1,0:T(8,128)S(1)}, s32[144,128]{1,0:T(8,128)S(1)}) custom-call(s32[8]{0:T(128)} %bitcast.11, s32[8]{0:T(128)} %zoff_ref.1, s32[8]{0:T(128)} %yoff_ref.1, f32[3,16,32,128]{3,2,1,0:T(8,128)} %velocity_ref.1, f32[16,32,128]{2,1,0:T(8,128)} %viscosity_ref.1, ...), custom_call_target="tpu_custom_call" | custom-call | tf_op jit(solution)/shard_map/pallas_call | solution.py:591
  21.1 4.8 %shard_map.87 = (f32[3,16,32,128]{3,2,1,0:T(8,128)}, f32[72,8,128]{2,1,0:T(8,128)S(1)}) custom-call(s32[144,128]{1,0:T(8,128)S(1)} %get-tuple-element.7.meta_ref, f32[144,8,128]{2,1,0:T(8,128)S(1)} %bitcast.6, f32[3,16,32,128]{3,2,1,0:T(8,128)S(1)} %get-tuple-element.9.moved_ref), custom_call_target="tpu_custom_call" | custom-call | tf_op jit(solution)/shard_map/pallas_call | solution.py:616
  25.9 14.9 %shard_map.88 = f32[3,8,128]{2,1,0:T(8,128)S(1)} custom-call(s32[8]{0:T(128)} %bitcast.12, f32[3,3,8,8,128]{4,3,2,1,0:T(8,128)S(1)} %bitcast.7), custom_call_target="tpu_custom_call" | custom-call | tf_op jit(solution)/shard_map/pallas_call | solution.py:634
  40.8 0.6 %copy.10 = f32[8,3,128]{2,0,1:T(8,128)} copy(f32[8,3,128]{2,0,1:T(8,128)S(1)} %bitcast.8) | data formatting | bytes 24576

commit v2 on v1

--- a/solution.py
+++ b/solution.py
@@ -12,7 +12,8 @@
 FAR = 4096.0
 ZP = 7
 YP = 8
-GROUP = 8
+PAIR = 16
+USED = 13
 TOGETHER = 4
 MESH = pl.DeviceIdType.MESH
 VMEM_LIMIT = 24 * 1024 * 1024
@@ -77,9 +78,43 @@
     return 0.5 * (visc + high), 0.5 * (visc + low)
 
 
+def make_list(depth, breadth, slots_ref, list_ref):
+    columns, length = slots_ref.shape[2], slots_ref.shape[4]
+    pairs, listed = 9 * columns, list_ref.shape[1]
+    rows = slots_ref[:, :, :, USED - 1 : USED, :].reshape(pairs, length)
+    number = lax.broadcasted_iota(jnp.int32, (pairs, length), 0)
+    lane = lax.broadcasted_iota(jnp.int32, (pairs, length), 1)
+    side, dr = number // (3 * columns), number // columns % 3
+    shift_z = ((dr - 1) * depth).astype(jnp.float32)
+    shift_y = jnp.where(side == 0, 0, jnp.where(side == 1, -breadth, breadth)).astype(jnp.float32)
+    earlier = lax.broadcasted_iota(jnp.int32, (pairs, pairs), 0) > lax.broadcasted_iota(
+        jnp.int32, (pairs, pairs), 1
+    )
+    earlier = earlier.astype(jnp.float32).astype(jnp.bfloat16)
+    place = lax.broadcasted_iota(jnp.int32, (pairs, listed), 1)
+    before = jnp.zeros((1, 1), jnp.float32)
+    listing = jnp.zeros((length, listed), jnp.float32)
+    for rank in range(CAP):
+        z = rows[:, 2 * rank : 2 * rank + 1] + shift_z
+        y = rows[:, 2 * rank + 1 : 2 * rank + 2] + shift_y
+        meets = (z > -BOX) & (z < depth) & (y > -BOX) & (y < breadth)
+        one = jnp.where(meets, 1.0, 0.0)
+        rank_of = jnp.dot(earlier, one.astype(jnp.bfloat16), preferred_element_type=jnp.float32) + before
+        spot = jnp.where(meets, rank_of, -1.0).astype(jnp.int32)
+        chosen = jnp.where(place == spot[:, 0:1], 1.0, 0.0).astype(jnp.bfloat16)
+        facts = jnp.where(lane == 0, z, jnp.where(lane == 1, y, jnp.where(lane == 2, number, 0).astype(jnp.float32)))
+        facts = jnp.where(meets, jnp.where(lane == 3, float(rank), facts), 0.0).astype(jnp.bfloat16)
+        listing = listing + lax.dot_general(
+            facts, chosen, (((0,), (0,)), ((), ())), preferred_element_type=jnp.float32
+        )
+        before = before + jnp.sum(one[:, 0:1], axis=0, keepdims=True)
+    list_ref[0:4, :] = listing[0:4].astype(jnp.int32)
+    list_ref[4:8, :] = jnp.broadcast_to(before, (4, listed)).astype(jnp.int32)
+
+
 def exchange_kernel(
     rows, columns, target_ref, zoff_ref, yoff_ref, velocity_ref, viscosity_ref, frac_ref, force_ref,
-    moved_ref, slots_ref, meta_ref,
+    field_ref, slots_ref, list_ref,
     pad, once, staging, layers_out, layers_in, corner_out, corner_in,
     load_sem, ab_send, ab_recv, halo_send, halo_recv, corner_send, corner_recv, c_send, c_recv,
 ):
@@ -102,15 +137,17 @@
     count = frac_ref.shape[1]
 
     def stage(column, unused):
+        row = jnp.full((1, length), FAR, jnp.float32)
         for rank, block in enumerate(matches(target_ref, count, column)):
             at = jnp.maximum(block, 0)
             there = block >= 0
             z = jnp.where(there, zoff_ref[at].astype(jnp.float32), FAR)
             y = jnp.where(there, yoff_ref[at].astype(jnp.float32), FAR)
-            staging[column, rank, 0:3, :] = frac_ref[:, at, :]
-            staging[column, rank, 3:6, :] = force_ref[:, at, :]
-            staging[column, rank, 6:7, :] = jnp.where(lanes == 0, z, y)
-            staging[column, rank, 7:8, :] = jnp.zeros((1, length), jnp.float32)
+            staging[column, 6 * rank : 6 * rank + 3, :] = frac_ref[:, at, :]
+            staging[column, 6 * rank + 3 : 6 * rank + 6, :] = force_ref[:, at, :]
+            row = jnp.where(lanes == 2 * rank, z, row)
+            row = jnp.where(lanes == 2 * rank + 1, y, row)
+        staging[column, 12:13, :] = row
         return unused
 
     lax.fori_loop(0, columns, stage, 0)
@@ -118,8 +155,8 @@
 
     def block_copy(dr, column):
         return pltpu.make_async_remote_copy(
-            src_ref=staging.at[column],
-            dst_ref=slots_ref.at[0, 1 - dr, xy],
+            src_ref=staging.at[column, 0:USED],
+            dst_ref=slots_ref.at[0, 1 - dr, xy, 0:USED],
             send_sem=ab_send.at[dr + 1],
             recv_sem=ab_recv.at[1 - dr],
             device_id=(gz + dr, column),
@@ -129,8 +166,8 @@
     def whole_row(dr):
         span = pl.ds(0, columns - (1 if dr == 0 else 0))
         return pltpu.make_async_remote_copy(
-            src_ref=staging.at[span],
-            dst_ref=slots_ref.at[0, dr + 1, span],
+            src_ref=staging.at[span, 0:USED],
+            dst_ref=slots_ref.at[0, dr + 1, span, 0:USED],
             send_sem=ab_send.at[dr + 1],
             recv_sem=ab_recv.at[dr + 1],
             device_id=(gz, xy),
@@ -139,7 +176,7 @@
 
     wait_greeting()
     each_peer(lambda dr, column: block_copy(dr, column).start())
-    slots_ref[0, 1, xy] = staging[xy]
+    slots_ref[0, 1, xy, 0:USED] = staging[xy, 0:USED]
 
     has = (gz > 0, gz < rows - 1, xy > 0, xy < columns - 1)
     device = ((gz - 1, xy), (gz + 1, xy), (gz, xy - 1), (gz, xy + 1))
@@ -177,6 +214,13 @@
     for side in (0, 1):
         on_side(side, lambda copy: copy.start())
 
+    wide, high = field_ref.shape[2], field_ref.shape[1]
+    field_ref[:, 0:ZP] = jnp.zeros((3, ZP, wide, length), jnp.float32)
+    field_ref[:, ZP + depth :] = jnp.zeros((3, high - ZP - depth, wide, length), jnp.float32)
+    field_ref[:, ZP : ZP + depth, 0:YP] = jnp.zeros((3, depth, YP, length), jnp.float32)
+    field_ref[:, ZP : ZP + depth, YP + breadth :] = jnp.zeros(
+        (3, depth, wide - YP - breadth, length), jnp.float32
+    )
     zeros_z = jnp.zeros((4, 2, breadth, length), jnp.float32)
     zeros_y = jnp.zeros((4, depth, 8, length), jnp.float32)
 
@@ -283,7 +327,7 @@
             cx_low,
         )
         for part in range(3):
-            moved_ref[part, z - 2] = laplace(
+            field_ref[part, z - 2 + ZP, YP : YP + breadth, :] = laplace(
                 once[part, z - 1, 8 : 8 + breadth, :], visc,
                 once[part, z - 2, 8 : 8 + breadth, :], once[part, z, 8 : 8 + breadth, :],
                 once[part, z - 1, 7 : 7 + breadth, :], once[part, z - 1, 9 : 9 + breadth, :],
@@ -316,8 +360,8 @@
     for number, (there, column, side) in enumerate(((has[3], xy + 1, 1), (has[2], xy - 1, 2))):
         for dr in (-1, 0, 1):
             copy = pltpu.make_async_remote_copy(
-                src_ref=slots_ref.at[0, dr + 1],
-                dst_ref=slots_ref.at[side, dr + 1],
+                src_ref=slots_ref.at[0, dr + 1, :, 0:USED],
+                dst_ref=slots_ref.at[side, dr + 1, :, 0:USED],
                 send_sem=c_send.at[number, dr + 1],
                 recv_sem=c_recv.at[number, dr + 1],
                 device_id=(gz, column),
@@ -361,15 +405,7 @@
 
     for unused, copy, dr, comes in forwards:
         pl.when(comes)(lambda copy=copy: copy.wait_recv())
-    for side in range(3):
-        for dr in range(3):
-            shift = jnp.where(lanes == 0, (dr - 1) * depth, (0, -breadth, breadth)[side])
-            for column in range(columns):
-                at = ((side * 3 + dr) * columns + column) * CAP
-                for rank in range(CAP):
-                    row = slots_ref[side, dr, column, rank, 6:7, :].astype(jnp.int32)
-                    meta_ref[at + rank : at + rank + 1, :] = row + shift
-
+    make_list(depth, breadth, slots_ref, list_ref)
     each_row(gz, rows, lambda dr: whole_row(dr).wait_send())
     for side in range(4):
         on_side(side, lambda copy: copy.wait_send())
@@ -393,43 +429,22 @@
 
 
 def product(left, right, contract):
-    dims = (((1,), (contract,)), ((), ()))
-    dot = functools.partial(
-        lax.dot_general, dimension_numbers=dims, preferred_element_type=jnp.float32
+    (left_high, left_low), (right_high, right_low) = left, right
+    return lax.dot_general(
+        jnp.concatenate([left_high, left_low, left_high], axis=1),
+        jnp.concatenate([right_high, right_high, right_low], axis=contract),
+        (((1,), (contract,)), ((), ())),
+        preferred_element_type=jnp.float32,
     )
-    (left_high, left_low), (right_high, right_low) = left, right
-    return dot(left_high, right_high) + dot(left_high, right_low) + dot(left_low, right_high)
 
 
 def points_kernel(
-    columns, meta_ref, slots_ref, moved_ref, new_ref, partial_ref, field, wx_high, wx_low, listed, load_sem, store_sem
+    depth, breadth, list_ref, slots_ref, field_in, new_ref, partial_ref, field, wx_high, wx_low, store_sem
 ):
-    depth, breadth, length = moved_ref.shape[1:]
-    inner = field.at[:, ZP : ZP + depth, YP : YP + breadth]
-    load = pltpu.make_async_copy(moved_ref, inner, load_sem)
-    load.start()
-    total_z = field.shape[1]
-    field[:, 0:ZP] = jnp.zeros((3, ZP) + field.shape[2:], jnp.float32)
-    field[:, ZP + depth :] = jnp.zeros((3, total_z - ZP - depth) + field.shape[2:], jnp.float32)
-    field[:, ZP : ZP + depth, 0:YP] = jnp.zeros((3, depth, YP, length), jnp.float32)
-    field[:, ZP : ZP + depth, YP + breadth :] = jnp.zeros(
-        (3, depth, field.shape[2] - YP - breadth, length), jnp.float32
-    )
+    length = field.shape[3]
     partial_ref[...] = jnp.zeros_like(partial_ref)
-    slot_count = meta_ref.shape[0]
-
-    def list_some(group, found):
-        for number in range(GROUP):
-            slot = group * GROUP + number
-            z, y = meta_ref[slot, 0], meta_ref[slot, 1]
-            meets = (z > -BOX) & (z < depth) & (y > -BOX) & (y < breadth)
-            listed[found] = slot
-            found = found + meets.astype(jnp.int32)
-        return found
-
-    found = lax.fori_loop(0, slot_count // GROUP, list_some, jnp.int32(0))
+    found = list_ref[4, 0]
     rounds = (found + TOGETHER - 1) // TOGETHER
-    load.wait()
 
     line = lax.broadcasted_iota(jnp.int32, (BOX, length), 0)
     rel = line.astype(jnp.float32)
@@ -438,26 +453,41 @@
     def members(number):
         for other in range(TOGETHER):
             at = number * TOGETHER + other
-            slot = listed[jnp.minimum(at, found - 1)]
-            yield at, at < found, slot, meta_ref[slot, 0], meta_ref[slot, 1]
-
-    def near_weights(tile, z, y):
-        wz = phi(2.0 + (BOX - 5) * tile[0:1] - rel)
-        wy = phi(2.0 + (BOX - 5) * tile[1:2] - rel)
+            spot = jnp.minimum(at, found - 1)
+            z, y, pair, rank = (list_ref[row, spot] for row in range(4))
+            yield at, at < found, pair, rank, z, y
+
+    def near_weights(frac, z, y):
+        wz = phi(2.0 + (BOX - 5) * frac[0:1] - rel)
+        wy = phi(2.0 + (BOX - 5) * frac[1:2] - rel)
         wz = jnp.where((z + line >= 0) & (z + line < depth), wz, 0.0)
         wy = jnp.where((y + line >= 0) & (y + line < breadth), wy, 0.0)
         return wz, wy
 
+    def far_weights(frac):
+        at = 2.0 + (length - 5) * frac
+        near = at - rel
+        base = phi(near - 4.0 * jnp.floor(0.25 * near + 0.5))
+        high = base.astype(jnp.bfloat16).astype(jnp.float32)
+        low = base - high
+        inside = jnp.abs(at - far) < 2.0
+
+        def spread_out(part):
+            whole = jnp.broadcast_to(part[None], (length // BOX, BOX, length)).reshape(length, length)
+            return jnp.where(inside, whole, 0.0).astype(jnp.bfloat16)
+
+        return spread_out(high), spread_out(low)
+
     def box_of(z, y):
         return (slice(None), pl.ds(z + ZP, BOX), pl.ds(y + YP, BOX), slice(None))
 
     def spread(number, unused):
         adds = []
-        for at, counts, slot, z, y in members(number):
-            tile = slots_ref[slot]
+        for at, counts, pair, rank, z, y in members(number):
+            tile = slots_ref[pair, pl.ds(6 * rank, 6), :]
             wz, wy = near_weights(tile, z, y)
             wy = jnp.where(counts, wy, 0.0)
-            wx = split(phi(2.0 + (length - 5) * tile[2:3] - far))
+            wx = far_weights(tile[2:3])
             wx_high[at], wx_low[at] = wx
             pulled = tile[3:6][:, None, :] * wz[None]
             coeff = pulled[:, :, None, :] * wy[None, None]
@@ -468,20 +498,22 @@
         return unused
 
     lax.fori_loop(0, rounds, spread, 0)
-    store = pltpu.make_async_copy(inner, new_ref, store_sem)
+    store = pltpu.make_async_copy(
+        field.at[:, ZP : ZP + depth, YP : YP + breadth], new_ref, store_sem
+    )
     store.start()
 
     def sample(number, unused):
         results = []
-        for at, counts, slot, z, y in members(number):
-            wz, wy = near_weights(slots_ref[slot], z, y)
+        for at, counts, pair, rank, z, y in members(number):
+            wz, wy = near_weights(slots_ref[pair, pl.ds(6 * rank, 6), :], z, y)
             cells = field[box_of(z, y)].reshape(3 * BOX * BOX, length)
             taken = product(split(cells), (wx_high[at], wx_low[at]), 0)
             taken = taken.reshape(3, BOX, BOX, length)
             summed = jnp.sum(taken * wz[None, :, None, :], axis=1)
-            results.append((slot, jnp.sum(summed * wy[None], axis=1)))
-        for slot, values in results:
-            partial_ref[slot // CAP, pl.ds(3 * lax.rem(slot, CAP), 3), :] = values
+            results.append((pair, rank, jnp.sum(summed * wy[None], axis=1)))
+        for pair, rank, values in results:
+            partial_ref[pair, pl.ds(3 * rank, 3), :] = values
         return unused
 
     lax.fori_loop(0, rounds, sample, 0)
@@ -587,20 +619,22 @@
     hbm = pl.BlockSpec(memory_space=pltpu.HBM)
     anyw = pl.BlockSpec(memory_space=pl.ANY)
     dma = pltpu.SemaphoreType.DMA
-    slot_count = 9 * columns * CAP
-    moved, slots, meta = pl.pallas_call(
+    pairs = 9 * columns
+    listed = pl.cdiv(CAP * pairs, length) * length
+    field_shape = (3, depth + 2 * ZP, breadth + 2 * YP, length)
+    field, slots, listing = pl.pallas_call(
         functools.partial(exchange_kernel, rows, columns),
         out_shape=(
-            jax.ShapeDtypeStruct(velocity.shape, f32),
-            jax.ShapeDtypeStruct((3, 3, columns, CAP, 8, length), f32),
-            jax.ShapeDtypeStruct((slot_count, length), jnp.int32),
+            jax.ShapeDtypeStruct(field_shape, f32),
+            jax.ShapeDtypeStruct((3, 3, columns, PAIR, length), f32),
+            jax.ShapeDtypeStruct((8, listed), jnp.int32),
         ),
         in_specs=[smem, smem, smem, hbm, hbm, vmem, vmem],
         out_specs=(vmem, vmem, vmem),
         scratch_shapes=[
             pltpu.VMEM((4, depth + 4, breadth + 16, length), f32),
             pltpu.VMEM((3, depth + 2, breadth + 16, length), f32),
-            pltpu.VMEM((columns, CAP, 8, length), f32),
+            pltpu.VMEM((columns, PAIR, length), f32),
             pltpu.VMEM((2, 4, 2 * depth, length), f32),
             pltpu.VMEM((2, 4, 2 * depth, length), f32),
             pltpu.VMEM((4, 8, length), f32),
@@ -613,23 +647,23 @@
         ),
     )(target, z_offset, y_offset, velocity, viscosity, frac, force)
 
-    new_velocity, partial = pl.pallas_call(
-        functools.partial(points_kernel, columns),
+    new_velocity, partial, unused = pl.pallas_call(
+        functools.partial(points_kernel, depth, breadth),
         out_shape=(
             jax.ShapeDtypeStruct(velocity.shape, f32),
-            jax.ShapeDtypeStruct((slot_count // CAP, 8, length), f32),
+            jax.ShapeDtypeStruct((pairs, 8, length), f32),
+            jax.ShapeDtypeStruct(field_shape, f32),
         ),
-        in_specs=[smem, vmem, anyw],
-        out_specs=(anyw, vmem),
+        in_specs=[smem, vmem, vmem],
+        out_specs=(anyw, vmem, vmem),
         scratch_shapes=[
-            pltpu.VMEM((3, depth + 2 * ZP, breadth + 2 * YP, length), f32),
-            pltpu.VMEM((slot_count + TOGETHER, length, length), jnp.bfloat16),
-            pltpu.VMEM((slot_count + TOGETHER, length, length), jnp.bfloat16),
-            pltpu.SMEM((slot_count + 1,), jnp.int32),
-            dma(()), dma(()),
+            pltpu.VMEM((CAP * pairs + TOGETHER, length, length), jnp.bfloat16),
+            pltpu.VMEM((CAP * pairs + TOGETHER, length, length), jnp.bfloat16),
+            dma(()),
         ],
+        input_output_aliases={2: 2},
         compiler_params=pltpu.CompilerParams(vmem_limit_bytes=VMEM_LIMIT),
-    )(meta, slots.reshape(slot_count, 8, length), moved)
+    )(listing, slots.reshape(pairs, PAIR, length), field)
 
     point_velocity = pl.pallas_call(
         functools.partial(return_kernel, rows, columns),

time: 41 us -> 38.5 us (0.939); the launches traced: 41.4 us -> 38.2 us
  Pallas kernels: 40.1 us -> 37 us
    pallas_call x1, Pallas kernels: 4.79 us -> 2.83 us  [shards(): pl.pallas_call(functools.partial(points_kernel, depth, breadth), out_shap...]
    pallas_call x1, Pallas kernels: 14.9 us -> 13.4 us  [shards(): pl.pallas_call(functools.partial(return_kernel, rows, columns), out_shape...]
where the time goes in v2:
time: 38.5 us; the launch traced here: 38.2 us
  Pallas kernels  37 us (96%)
  between operations  0.66 us (2%)
  local copies, waits for them, and re-layouts  0.6 us (2%)
    pallas_call x1, Pallas kernels, shards(): pl.pallas_call(functools.partial(exchange_kernel, rows, columns), out_sha...  20.8 us
    pallas_call x1, Pallas kernels, shards(): pl.pallas_call(functools.partial(return_kernel, rows, columns), out_shape...  13.4 us
    pallas_call x1, Pallas kernels, shards(): pl.pallas_call(functools.partial(points_kernel, depth, breadth), out_shap...  2.83 us

profile of v2, /device:TPU:0, one launch (start us, length us, event | category | flops | bytes accessed | tf_op | source)
XLA Modules:
  0.0 38.2 jit_solution(17925803048291971803)
XLA Ops:
  0.6 20.8 %shard_map.86 = (f32[3,30,48,128]{3,2,1,0:T(8,128)S(1)}, f32[3,3,8,16,128]{4,3,2,1,0:T(8,128)S(1)}, s32[8,256]{1,0:T(8,128)S(1)}) custom-call(s32[8]{0:T(128)} %bitcast.11, s32[8]{0:T(128)} %zoff_ref.1, s32[8]{0:T(128)} %yoff_ref.1, f32[3,16,32,128]{3,2,1,0:T(8,128)} %velocity_ref.1, f32[16,32,128]{2,1,0:T(8,128)} %viscosity_ref.1, f32[3,8,128]{2,1,0:T(8,128)} %bitcast.9, ...), custom_call_target="tpu_custom_call" | custom-call | tf_op jit(solution)/shard_map/pallas_call | solution.py:625
  21.4 2.8 %shard_map.87 = (f32[3,16,32,128]{3,2,1,0:T(8,128)}, f32[72,8,128]{2,1,0:T(8,128)S(1)}, f32[3,30,48,128]{3,2,1,0:T(8,128)S(1)}) custom-call(s32[8,256]{1,0:T(8,128)S(1)} %get-tuple-element.7.list_ref, f32[72,16,128]{2,1,0:T(8,128)S(1)} %bitcast.6, f32[3,30,48,128]{3,2,1,0:T(8,128)S(1)} %get-tuple-element.9.field_in), custom_call_target="tpu_custom_call", output_to_operand_aliasing={{2}: (2, {})} | custom-call | tf_op jit(solution)/shard_map/pallas_call | solution.py:650
  24.2 13.4 %shard_map.88 = f32[3,8,128]{2,1,0:T(8,128)S(1)} custom-call(s32[8]{0:T(128)} %bitcast.12, f32[3,3,8,8,128]{4,3,2,1,0:T(8,128)S(1)} %bitcast.7), custom_call_target="tpu_custom_call" | custom-call | tf_op jit(solution)/shard_map/pallas_call | solution.py:668
  37.6 0.6 %copy.12 = f32[8,3,128]{2,0,1:T(8,128)} copy(f32[8,3,128]{2,0,1:T(8,128)S(1)} %bitcast.8) | data formatting | bytes 24576

commit v3 on v2

--- a/solution.py
+++ b/solution.py
@@ -15,6 +15,7 @@
 PAIR = 16
 USED = 13
 TOGETHER = 4
+CORES = 2
 MESH = pl.DeviceIdType.MESH
 VMEM_LIMIT = 24 * 1024 * 1024
 
@@ -50,6 +51,24 @@
         1 + (gz > 0).astype(jnp.int32) + (gz < rows - 1).astype(jnp.int32)
     )
     return lambda: pl.semaphore_wait(barrier, near * columns - 1)
+
+
+def chip_peers(gz, xy, rows, columns, steps):
+    chip, core = xy // CORES, xy % CORES
+    chips = columns // CORES
+
+    def each(body):
+        for step in steps:
+            for dr in (0, -1, 1):
+                there = (gz + dr >= 0) & (gz + dr < rows) & (chip + step >= 0) & (chip + step < chips)
+                for turn in range(CORES):
+                    if step == 0 and dr == 0 and turn == 0:
+                        continue
+                    other = core + turn
+                    column = (chip + step) * CORES + jnp.where(other >= CORES, other - CORES, other)
+                    pl.when(there)(functools.partial(body, dr, column))
+
+    return each
 
 
 def matches(target_ref, count, column):
@@ -116,12 +135,21 @@
     rows, columns, target_ref, zoff_ref, yoff_ref, velocity_ref, viscosity_ref, frac_ref, force_ref,
     field_ref, slots_ref, list_ref,
     pad, once, staging, layers_out, layers_in, corner_out, corner_in,
-    load_sem, ab_send, ab_recv, halo_send, halo_recv, corner_send, corner_recv, c_send, c_recv,
+    load_sem, ab_send, ab_recv, halo_send, halo_recv, corner_send, corner_recv, c_send, c_recv, known,
 ):
     gz, xy = lax.axis_index("gz"), lax.axis_index("xy")
     depth, breadth = velocity_ref.shape[1], velocity_ref.shape[2]
     length = velocity_ref.shape[3]
-    wait_greeting = greet(gz, xy, rows, columns)
+    chip, chips = xy // CORES, columns // CORES
+    barrier = pltpu.get_barrier_semaphore()
+    near_peers = chip_peers(gz, xy, rows, columns, (0, -1, 1))
+
+    def signal_near(dr, column):
+        pl.semaphore_signal(barrier, inc=1, device_id=(gz + dr, column), device_id_type=MESH)
+
+    near_peers(signal_near)
+    near_rows = 1 + (gz > 0).astype(jnp.int32) + (gz < rows - 1).astype(jnp.int32)
+    near_chips = 1 + (chip > 0).astype(jnp.int32) + (chip < chips - 1).astype(jnp.int32)
     loads = (
         pltpu.make_async_copy(
             velocity_ref, pad.at[0:3, 2 : 2 + depth, 8 : 8 + breadth], load_sem.at[0]
@@ -151,8 +179,6 @@
         return unused
 
     lax.fori_loop(0, columns, stage, 0)
-    each_peer = peers(gz, xy, rows, columns)
-
     def block_copy(dr, column):
         return pltpu.make_async_remote_copy(
             src_ref=staging.at[column, 0:USED],
@@ -174,8 +200,22 @@
             device_id_type=MESH,
         )
 
-    wait_greeting()
-    each_peer(lambda dr, column: block_copy(dr, column).start())
+    def tell(stage):
+        for number, (there, column) in enumerate(chain):
+            pl.when(there)(
+                lambda number=number, column=column: pl.semaphore_signal(
+                    known.at[stage, number], inc=1, device_id=(gz, column), device_id_type=MESH
+                )
+            )
+
+    def hear(stage):
+        for number, (there, column) in enumerate(chain):
+            pl.when(there)(lambda number=number: pl.semaphore_wait(known.at[stage, 1 - number], 1))
+
+    chain = ((chip < chips - 1, xy + CORES), (chip > 0, xy - CORES))
+    pl.semaphore_wait(barrier, near_rows * near_chips * CORES - 1)
+    tell(0)
+    near_peers(lambda dr, column: block_copy(dr, column).start())
     slots_ref[0, 1, xy, 0:USED] = staging[xy, 0:USED]
 
     has = (gz > 0, gz < rows - 1, xy > 0, xy < columns - 1)
@@ -214,6 +254,13 @@
     for side in (0, 1):
         on_side(side, lambda copy: copy.start())
 
+    for stage in range(chips - 2):
+        hear(stage)
+        if stage < chips - 3:
+            tell(stage + 1)
+        far_peers = chip_peers(gz, xy, rows, columns, (-2 - stage, 2 + stage))
+        far_peers(lambda dr, column: block_copy(dr, column).start())
+
     wide, high = field_ref.shape[2], field_ref.shape[1]
     field_ref[:, 0:ZP] = jnp.zeros((3, ZP, wide, length), jnp.float32)
     field_ref[:, ZP + depth :] = jnp.zeros((3, high - ZP - depth, wide, length), jnp.float32)
@@ -374,15 +421,17 @@
             if dr == row:
                 pl.when(there)(lambda copy=copy: copy.start())
 
+    wait_side(2, 3)
+    wait_side(3, 2)
+    loop(3, 1 + depth, first_sweep)
     whole_row(0).wait_recv()
     forward(0)
-    wait_side(2, 3)
-    wait_side(3, 2)
-    loop(3, 3 + depth // 4, first_sweep)
+    middle = 4 + (depth - 4) // 2
+    loop(4, middle, second_sweep)
     for dr in (-1, 1):
         pl.when(has[0 if dr < 0 else 1])(lambda dr=dr: whole_row(dr).wait_recv())
         forward(dr)
-    loop(3 + depth // 4, 1 + depth, first_sweep)
+    loop(middle, depth, second_sweep)
 
     wait_side(0, 1)
     wait_side(1, 0)
@@ -401,7 +450,8 @@
 
     for z in (1, 2, 1 + depth, 2 + depth):
         first_sweep(z)
-    loop(2, 2 + depth, second_sweep)
+    for z in (2, 3, depth, 1 + depth):
+        second_sweep(z)
 
     for unused, copy, dr, comes in forwards:
         pl.when(comes)(lambda copy=copy: copy.wait_recv())
@@ -641,6 +691,7 @@
             pltpu.VMEM((4, 8, length), f32),
             dma((2,)), dma((3,)), dma((3,)), dma((4, 2)), dma((4, 2)),
             dma((4,)), dma((4,)), dma((2, 3)), dma((2, 3)),
+            pltpu.SemaphoreType.REGULAR((max(columns // CORES - 2, 1), 2)),
         ],
         compiler_params=pltpu.CompilerParams(
             collective_id=0, has_side_effects=True, vmem_limit_bytes=VMEM_LIMIT

time: 38.5 us -> 36.5 us (0.948); the launches traced: 38.2 us -> 35.8 us
  Pallas kernels: 37 us -> 34.6 us
    pallas_call x1, Pallas kernels: 20.8 us -> 16.9 us  [shards(): pl.pallas_call(functools.partial(exchange_kernel, rows, columns), out_sha...]
    pallas_call x1, Pallas kernels: 13.4 us -> 14.9 us  [shards(): pl.pallas_call(functools.partial(return_kernel, rows, columns), out_shape...]
where the time goes in v3:
time: 36.5 us; the launch traced here: 35.8 us
  Pallas kernels  34.6 us (95%)
  between operations  0.66 us (2%)
  local copies, waits for them, and re-layouts  0.6 us (2%)
    pallas_call x1, Pallas kernels, shards(): pl.pallas_call(functools.partial(exchange_kernel, rows, columns), out_sha...  16.9 us
    pallas_call x1, Pallas kernels, shards(): pl.pallas_call(functools.partial(return_kernel, rows, columns), out_shape...  14.9 us
    pallas_call x1, Pallas kernels, shards(): pl.pallas_call(functools.partial(points_kernel, depth, breadth), out_shap...  2.83 us

profile of v3, /device:TPU:0, one launch (start us, length us, event | category | flops | bytes accessed | tf_op | source)
XLA Modules:
  0.0 35.8 jit_solution(12391821534461248677)
XLA Ops:
  0.6 16.9 %shard_map.86 = (f32[3,30,48,128]{3,2,1,0:T(8,128)S(1)}, f32[3,3,8,16,128]{4,3,2,1,0:T(8,128)S(1)}, s32[8,256]{1,0:T(8,128)S(1)}) custom-call(s32[8]{0:T(128)} %bitcast.11, s32[8]{0:T(128)} %zoff_ref.1, s32[8]{0:T(128)} %yoff_ref.1, f32[3,16,32,128]{3,2,1,0:T(8,128)} %velocity_ref.1, f32[16,32,128]{2,1,0:T(8,128)} %viscosity_ref.1, f32[3,8,128]{2,1,0:T(8,128)} %bitcast.9, ...), custom_call_target="tpu_custom_call" | custom-call | tf_op jit(solution)/shard_map/pallas_call | solution.py:675
  17.5 2.8 %shard_map.87 = (f32[3,16,32,128]{3,2,1,0:T(8,128)}, f32[72,8,128]{2,1,0:T(8,128)S(1)}, f32[3,30,48,128]{3,2,1,0:T(8,128)S(1)}) custom-call(s32[8,256]{1,0:T(8,128)S(1)} %get-tuple-element.7.list_ref, f32[72,16,128]{2,1,0:T(8,128)S(1)} %bitcast.6, f32[3,30,48,128]{3,2,1,0:T(8,128)S(1)} %get-tuple-element.9.field_in), custom_call_target="tpu_custom_call", output_to_operand_aliasing={{2}: (2, {})} | custom-call | tf_op jit(solution)/shard_map/pallas_call | solution.py:701
  20.3 14.9 %shard_map.88 = f32[3,8,128]{2,1,0:T(8,128)S(1)} custom-call(s32[8]{0:T(128)} %bitcast.12, f32[3,3,8,8,128]{4,3,2,1,0:T(8,128)S(1)} %bitcast.7), custom_call_target="tpu_custom_call" | custom-call | tf_op jit(solution)/shard_map/pallas_call | solution.py:719
  35.2 0.6 %copy.12 = f32[8,3,128]{2,0,1:T(8,128)} copy(f32[8,3,128]{2,0,1:T(8,128)S(1)} %bitcast.8) | data formatting | bytes 24576

commit v4 on v3

--- a/solution.py
+++ b/solution.py
@@ -14,43 +14,17 @@
 YP = 8
 PAIR = 16
 USED = 13
+KEPT = 6
 TOGETHER = 4
 CORES = 2
 MESH = pl.DeviceIdType.MESH
 VMEM_LIMIT = 24 * 1024 * 1024
 
 
-def peers(gz, xy, rows, columns):
-    def each(body):
-        for dr in (-1, 0, 1):
-            inside = jnp.logical_and(gz + dr >= 0, gz + dr < rows)
-
-            @pl.when(inside)
-            def _(dr=dr):
-                for k in range(1 if dr == 0 else 0, columns):
-                    column = xy + k
-                    body(dr, jnp.where(column >= columns, column - columns, column))
-
-    return each
-
-
 def each_row(gz, rows, body):
     for dr in (-1, 0, 1):
         inside = jnp.logical_and(gz + dr >= 0, gz + dr < rows)
         pl.when(inside)(functools.partial(body, dr))
-
-
-def greet(gz, xy, rows, columns):
-    barrier = pltpu.get_barrier_semaphore()
-
-    def signal(dr, column):
-        pl.semaphore_signal(barrier, inc=1, device_id=(gz + dr, column), device_id_type=MESH)
-
-    peers(gz, xy, rows, columns)(signal)
-    near = (
-        1 + (gz > 0).astype(jnp.int32) + (gz < rows - 1).astype(jnp.int32)
-    )
-    return lambda: pl.semaphore_wait(barrier, near * columns - 1)
 
 
 def chip_peers(gz, xy, rows, columns, steps):
@@ -71,6 +45,51 @@
     return each
 
 
+def staged_greeting(gz, xy, rows, columns, known):
+    chip, chips = xy // CORES, columns // CORES
+    barrier = pltpu.get_barrier_semaphore()
+    near_peers = chip_peers(gz, xy, rows, columns, (0, -1, 1))
+
+    def signal_near(dr, column):
+        pl.semaphore_signal(barrier, inc=1, device_id=(gz + dr, column), device_id_type=MESH)
+
+    near_peers(signal_near)
+    near_rows = 1 + (gz > 0).astype(jnp.int32) + (gz < rows - 1).astype(jnp.int32)
+    near_chips = 1 + (chip > 0).astype(jnp.int32) + (chip < chips - 1).astype(jnp.int32)
+    chain = ((chip < chips - 1, xy + CORES), (chip > 0, xy - CORES))
+
+    def tell(reach):
+        for number, (there, column) in enumerate(chain):
+            pl.when(there)(
+                lambda number=number, column=column: pl.semaphore_signal(
+                    known.at[reach, number], inc=1, device_id=(gz, column), device_id_type=MESH
+                )
+            )
+
+    def hear(reach):
+        for number, (there, column) in enumerate(chain):
+            pl.when(there)(lambda number=number: pl.semaphore_wait(known.at[reach, 1 - number], 1))
+
+    def near():
+        pl.semaphore_wait(barrier, near_rows * near_chips * CORES - 1)
+        if chips > 2:
+            tell(0)
+        return near_peers
+
+    def farther():
+        for reach in range(chips - 2):
+            hear(reach)
+            if reach < chips - 3:
+                tell(reach + 1)
+            yield chip_peers(gz, xy, rows, columns, (-2 - reach, 2 + reach))
+
+    return near, farther
+
+
+def known_shape(columns):
+    return pltpu.SemaphoreType.REGULAR((max(columns // CORES - 2, 1), 2))
+
+
 def matches(target_ref, count, column):
     first, second = jnp.int32(-1), jnp.int32(-1)
     for j in range(count):
@@ -101,55 +120,56 @@
     columns, length = slots_ref.shape[2], slots_ref.shape[4]
     pairs, listed = 9 * columns, list_ref.shape[1]
     rows = slots_ref[:, :, :, USED - 1 : USED, :].reshape(pairs, length)
-    number = lax.broadcasted_iota(jnp.int32, (pairs, length), 0)
-    lane = lax.broadcasted_iota(jnp.int32, (pairs, length), 1)
-    side, dr = number // (3 * columns), number // columns % 3
-    shift_z = ((dr - 1) * depth).astype(jnp.float32)
-    shift_y = jnp.where(side == 0, 0, jnp.where(side == 1, -breadth, breadth)).astype(jnp.float32)
-    earlier = lax.broadcasted_iota(jnp.int32, (pairs, pairs), 0) > lax.broadcasted_iota(
+    facts = jnp.transpose(rows)[0:8]
+    number = lax.broadcasted_iota(jnp.int32, (1, pairs), 1)
+    above = (number >= 3 * columns).astype(jnp.int32)
+    below = (number >= 6 * columns).astype(jnp.int32)
+    place = number - 3 * columns * (above + below)
+    level = (place >= columns).astype(jnp.int32) + (place >= 2 * columns).astype(jnp.int32)
+    shift_z = ((level - 1) * depth).astype(jnp.float32)
+    shift_y = ((2 * below - above) * breadth).astype(jnp.float32)
+    earlier = lax.broadcasted_iota(jnp.int32, (pairs, pairs), 0) < lax.broadcasted_iota(
         jnp.int32, (pairs, pairs), 1
     )
     earlier = earlier.astype(jnp.float32).astype(jnp.bfloat16)
-    place = lax.broadcasted_iota(jnp.int32, (pairs, listed), 1)
-    before = jnp.zeros((1, 1), jnp.float32)
-    listing = jnp.zeros((length, listed), jnp.float32)
+    found = []
     for rank in range(CAP):
-        z = rows[:, 2 * rank : 2 * rank + 1] + shift_z
-        y = rows[:, 2 * rank + 1 : 2 * rank + 2] + shift_y
+        z = facts[2 * rank : 2 * rank + 1] + shift_z
+        y = facts[2 * rank + 1 : 2 * rank + 2] + shift_y
         meets = (z > -BOX) & (z < depth) & (y > -BOX) & (y < breadth)
-        one = jnp.where(meets, 1.0, 0.0)
-        rank_of = jnp.dot(earlier, one.astype(jnp.bfloat16), preferred_element_type=jnp.float32) + before
-        spot = jnp.where(meets, rank_of, -1.0).astype(jnp.int32)
-        chosen = jnp.where(place == spot[:, 0:1], 1.0, 0.0).astype(jnp.bfloat16)
-        facts = jnp.where(lane == 0, z, jnp.where(lane == 1, y, jnp.where(lane == 2, number, 0).astype(jnp.float32)))
-        facts = jnp.where(meets, jnp.where(lane == 3, float(rank), facts), 0.0).astype(jnp.bfloat16)
+        found.append((z, y, meets, jnp.where(meets, 1.0, 0.0)))
+    both = found[0][3] + found[1][3]
+    spot = jnp.dot(
+        jnp.broadcast_to(both, (BOX, pairs)).astype(jnp.bfloat16), earlier,
+        preferred_element_type=jnp.float32,
+    )[0:1]
+    entry = lax.broadcasted_iota(jnp.int32, (listed, pairs), 0).astype(jnp.float32)
+    fact = lax.broadcasted_iota(jnp.int32, (BOX, pairs), 0)
+    listing = jnp.zeros((BOX, listed), jnp.float32)
+    for rank, (z, y, meets, one) in enumerate(found):
+        mine = jnp.where(meets, spot + (found[0][3] if rank else 0.0), -1.0)
+        chosen = jnp.where(entry == mine, 1.0, 0.0).astype(jnp.bfloat16)
+        told = jnp.where(fact == 0, z, jnp.where(fact == 1, y, number.astype(jnp.float32)))
+        told = jnp.where(meets, jnp.where(fact == 3, float(rank), told), 0.0).astype(jnp.bfloat16)
         listing = listing + lax.dot_general(
-            facts, chosen, (((0,), (0,)), ((), ())), preferred_element_type=jnp.float32
-        )
-        before = before + jnp.sum(one[:, 0:1], axis=0, keepdims=True)
+            told, chosen, (((1,), (1,)), ((), ())), preferred_element_type=jnp.float32
+        )
     list_ref[0:4, :] = listing[0:4].astype(jnp.int32)
-    list_ref[4:8, :] = jnp.broadcast_to(before, (4, listed)).astype(jnp.int32)
+    total = jnp.sum(both, axis=1, keepdims=True)
+    list_ref[4:8, :] = jnp.broadcast_to(total, (4, listed)).astype(jnp.int32)
 
 
 def exchange_kernel(
-    rows, columns, target_ref, zoff_ref, yoff_ref, velocity_ref, viscosity_ref, frac_ref, force_ref,
+    rows, columns, target_hbm, zoff_hbm, yoff_hbm, velocity_ref, viscosity_ref, frac_hbm, force_hbm,
     field_ref, slots_ref, list_ref,
     pad, once, staging, layers_out, layers_in, corner_out, corner_in,
     load_sem, ab_send, ab_recv, halo_send, halo_recv, corner_send, corner_recv, c_send, c_recv, known,
+    target_ref, zoff_ref, yoff_ref, frac_ref, force_ref, small_sem,
 ):
     gz, xy = lax.axis_index("gz"), lax.axis_index("xy")
     depth, breadth = velocity_ref.shape[1], velocity_ref.shape[2]
     length = velocity_ref.shape[3]
-    chip, chips = xy // CORES, columns // CORES
-    barrier = pltpu.get_barrier_semaphore()
-    near_peers = chip_peers(gz, xy, rows, columns, (0, -1, 1))
-
-    def signal_near(dr, column):
-        pl.semaphore_signal(barrier, inc=1, device_id=(gz + dr, column), device_id_type=MESH)
-
-    near_peers(signal_near)
-    near_rows = 1 + (gz > 0).astype(jnp.int32) + (gz < rows - 1).astype(jnp.int32)
-    near_chips = 1 + (chip > 0).astype(jnp.int32) + (chip < chips - 1).astype(jnp.int32)
+    near, farther = staged_greeting(gz, xy, rows, columns, known)
     loads = (
         pltpu.make_async_copy(
             velocity_ref, pad.at[0:3, 2 : 2 + depth, 8 : 8 + breadth], load_sem.at[0]
@@ -158,6 +178,15 @@
             viscosity_ref, pad.at[3, 2 : 2 + depth, 8 : 8 + breadth], load_sem.at[1]
         ),
     )
+    small = [
+        pltpu.make_async_copy(source, place, small_sem.at[number])
+        for number, (source, place) in enumerate((
+            (target_hbm, target_ref), (zoff_hbm, zoff_ref), (yoff_hbm, yoff_ref),
+            (frac_hbm, frac_ref), (force_hbm, force_ref),
+        ))
+    ]
+    for load in small:
+        load.start()
     for load in loads:
         load.start()
 
@@ -178,7 +207,6 @@
         staging[column, 12:13, :] = row
         return unused
 
-    lax.fori_loop(0, columns, stage, 0)
     def block_copy(dr, column):
         return pltpu.make_async_remote_copy(
             src_ref=staging.at[column, 0:USED],
@@ -200,23 +228,10 @@
             device_id_type=MESH,
         )
 
-    def tell(stage):
-        for number, (there, column) in enumerate(chain):
-            pl.when(there)(
-                lambda number=number, column=column: pl.semaphore_signal(
-                    known.at[stage, number], inc=1, device_id=(gz, column), device_id_type=MESH
-                )
-            )
-
-    def hear(stage):
-        for number, (there, column) in enumerate(chain):
-            pl.when(there)(lambda number=number: pl.semaphore_wait(known.at[stage, 1 - number], 1))
-
-    chain = ((chip < chips - 1, xy + CORES), (chip > 0, xy - CORES))
-    pl.semaphore_wait(barrier, near_rows * near_chips * CORES - 1)
-    tell(0)
-    near_peers(lambda dr, column: block_copy(dr, column).start())
-    slots_ref[0, 1, xy, 0:USED] = staging[xy, 0:USED]
+    for load in small:
+        load.wait()
+    lax.fori_loop(0, columns, stage, 0)
+    near_peers = near()
 
     has = (gz > 0, gz < rows - 1, xy > 0, xy < columns - 1)
     device = ((gz - 1, xy), (gz + 1, xy), (gz, xy - 1), (gz, xy + 1))
@@ -251,15 +266,12 @@
             for copy in halo_copies(side):
                 action(copy)
 
+
+    near_peers(lambda dr, column: block_copy(dr, column).start())
+    slots_ref[0, 1, xy, 0:USED] = staging[xy, 0:USED]
     for side in (0, 1):
         on_side(side, lambda copy: copy.start())
 
-    for stage in range(chips - 2):
-        hear(stage)
-        if stage < chips - 3:
-            tell(stage + 1)
-        far_peers = chip_peers(gz, xy, rows, columns, (-2 - stage, 2 + stage))
-        far_peers(lambda dr, column: block_copy(dr, column).start())
 
     wide, high = field_ref.shape[2], field_ref.shape[1]
     field_ref[:, 0:ZP] = jnp.zeros((3, ZP, wide, length), jnp.float32)
@@ -330,6 +342,9 @@
     for present, copy, arrival, number, z_out, y_out in corners:
         pl.when(present)(lambda copy=copy: copy.start())
 
+    for far_peers in farther():
+        far_peers(lambda dr, column: block_copy(dr, column).start())
+
     lane = lax.broadcasted_iota(jnp.int32, (breadth + 16, length), 1)
     line = lax.broadcasted_iota(jnp.int32, (breadth + 16, length), 0)
     low_y = jnp.where(xy > 0, 0, 8)
@@ -571,49 +586,40 @@
 
 
 def return_kernel(
-    rows, columns, target_ref, partial_ref, out_ref,
-    side_in, summed, gathered, c_send, c_recv, ab_send, ab_recv,
+    rows, columns, target_hbm, partial_ref, out_ref,
+    side_in, summed, gathered, c_send, c_recv, ab_send, ab_recv, known, target_ref, target_sem,
 ):
     gz, xy = lax.axis_index("gz"), lax.axis_index("xy")
-    wait_greeting = greet(gz, xy, rows, columns)
-    wait_greeting()
+    near, farther = staged_greeting(gz, xy, rows, columns, known)
+    target_load = pltpu.make_async_copy(target_hbm, target_ref, target_sem)
+    target_load.start()
     has_low, has_high = xy > 0, xy < columns - 1
-    copies = []
-    for number, (there, column) in enumerate(((has_low, xy - 1), (has_high, xy + 1))):
-        copy = pltpu.make_async_remote_copy(
-            src_ref=partial_ref.at[number + 1],
-            dst_ref=side_in.at[1 - number],
+    sides = ((has_low, xy - 1), (has_high, xy + 1))
+
+    def side_copy(number, column, landing):
+        return pltpu.make_async_remote_copy(
+            src_ref=partial_ref.at[number + 1, :, :, 0:KEPT],
+            dst_ref=side_in.at[landing, :, :, 0:KEPT],
             send_sem=c_send.at[number],
-            recv_sem=c_recv.at[1 - number],
+            recv_sem=c_recv.at[landing],
             device_id=(gz, column),
             device_id_type=MESH,
         )
-        arrival = pltpu.make_async_remote_copy(
-            src_ref=partial_ref.at[number + 1],
-            dst_ref=side_in.at[number],
-            send_sem=c_send.at[number],
-            recv_sem=c_recv.at[number],
-            device_id=(gz, column),
-            device_id_type=MESH,
-        )
-        copies.append((there, copy))
-        pl.when(there)(lambda copy=copy: copy.start())
+
+    near_peers = near()
+    for number, (there, column) in enumerate(sides):
+        pl.when(there)(
+            lambda number=number, column=column: side_copy(number, column, 1 - number).start()
+        )
 
         @pl.when(jnp.logical_not(there))
         def _(number=number):
             side_in[number] = jnp.zeros(side_in.shape[1:], jnp.float32)
 
-        copies[-1] = (there, copy, arrival)
-    for there, copy, arrival in copies:
-        pl.when(there)(lambda arrival=arrival: arrival.wait_recv())
-    summed[...] = partial_ref[0] + side_in[0] + side_in[1]
-
-    each_peer = peers(gz, xy, rows, columns)
-
     def block_copy(dr, column):
         return pltpu.make_async_remote_copy(
-            src_ref=summed.at[dr + 1, column],
-            dst_ref=gathered.at[1 - dr, xy],
+            src_ref=summed.at[dr + 1, column, 0:KEPT],
+            dst_ref=gathered.at[1 - dr, xy, 0:KEPT],
             send_sem=ab_send.at[dr + 1],
             recv_sem=ab_recv.at[1 - dr],
             device_id=(gz + dr, column),
@@ -623,17 +629,14 @@
     def whole_row(dr):
         span = pl.ds(0, columns - (1 if dr == 0 else 0))
         return pltpu.make_async_remote_copy(
-            src_ref=summed.at[dr + 1, span],
-            dst_ref=gathered.at[dr + 1, span],
+            src_ref=summed.at[dr + 1, span, 0:KEPT],
+            dst_ref=gathered.at[dr + 1, span, 0:KEPT],
             send_sem=ab_send.at[dr + 1],
             recv_sem=ab_recv.at[dr + 1],
             device_id=(gz, xy),
             device_id_type=MESH,
         )
 
-    each_peer(lambda dr, column: block_copy(dr, column).start())
-    gathered[1, xy] = summed[1, xy]
-
     @pl.when(gz == 0)
     def _():
         gathered[0] = jnp.zeros(gathered.shape[1:], jnp.float32)
@@ -642,18 +645,36 @@
     def _():
         gathered[2] = jnp.zeros(gathered.shape[1:], jnp.float32)
 
-    each_row(gz, rows, lambda dr: whole_row(dr).wait_recv())
+    far_peers = list(farther())
+    for number, (there, column) in enumerate(sides):
+        pl.when(there)(
+            lambda number=number, column=column: side_copy(number, column, number).wait_recv()
+        )
+    summed[:, :, 0:KEPT] = (
+        partial_ref[0, :, :, 0:KEPT] + side_in[0, :, :, 0:KEPT] + side_in[1, :, :, 0:KEPT]
+    )
+    for group in far_peers[::-1] + [near_peers]:
+        group(lambda dr, column: block_copy(dr, column).start())
+    gathered[1, xy, 0:KEPT] = summed[1, xy, 0:KEPT]
+
+    target_load.wait()
     count = out_ref.shape[1]
+    ranks = []
     for j in range(count):
-        column = target_ref[j]
         rank = jnp.int32(0)
         for earlier in range(j):
-            rank = rank + (target_ref[earlier] == column).astype(jnp.int32)
+            rank = rank + (target_ref[earlier] == target_ref[j]).astype(jnp.int32)
+        ranks.append(rank)
+    each_row(gz, rows, lambda dr: whole_row(dr).wait_recv())
+    for j, rank in enumerate(ranks):
+        column = target_ref[j]
         tile = gathered[0, column] + gathered[1, column] + gathered[2, column]
-        out_ref[:, j, :] = jnp.where(rank == 0, tile[0:3], tile[3:6])
+        out_ref[:, j, :] = jnp.where(rank == 0, tile[0:3], tile[3:KEPT])
     each_row(gz, rows, lambda dr: whole_row(dr).wait_send())
-    for there, copy, arrival in copies:
-        pl.when(there)(lambda copy=copy: copy.wait_send())
+    for number, (there, column) in enumerate(sides):
+        pl.when(there)(
+            lambda number=number, column=column: side_copy(number, column, number).wait_send()
+        )
 
 
 def shards(rows, columns, velocity, viscosity, frac, force, target, z_offset, y_offset):
@@ -679,7 +700,7 @@
             jax.ShapeDtypeStruct((3, 3, columns, PAIR, length), f32),
             jax.ShapeDtypeStruct((8, listed), jnp.int32),
         ),
-        in_specs=[smem, smem, smem, hbm, hbm, vmem, vmem],
+        in_specs=[hbm] * 7,
         out_specs=(vmem, vmem, vmem),
         scratch_shapes=[
             pltpu.VMEM((4, depth + 4, breadth + 16, length), f32),
@@ -691,7 +712,13 @@
             pltpu.VMEM((4, 8, length), f32),
             dma((2,)), dma((3,)), dma((3,)), dma((4, 2)), dma((4, 2)),
             dma((4,)), dma((4,)), dma((2, 3)), dma((2, 3)),
-            pltpu.SemaphoreType.REGULAR((max(columns // CORES - 2, 1), 2)),
+            known_shape(columns),
+            pltpu.SMEM(target.shape, jnp.int32),
+            pltpu.SMEM(target.shape, jnp.int32),
+            pltpu.SMEM(target.shape, jnp.int32),
+            pltpu.VMEM(frac.shape, f32),
+            pltpu.VMEM(force.shape, f32),
+            dma((5,)),
         ],
         compiler_params=pltpu.CompilerParams(
             collective_id=0, has_side_effects=True, vmem_limit_bytes=VMEM_LIMIT
@@ -719,13 +746,14 @@
     point_velocity = pl.pallas_call(
         functools.partial(return_kernel, rows, columns),
         out_shape=jax.ShapeDtypeStruct(frac.shape, f32),
-        in_specs=[smem, vmem],
+        in_specs=[hbm, vmem],
         out_specs=vmem,
         scratch_shapes=[
             pltpu.VMEM((2, 3, columns, 8, length), f32),
             pltpu.VMEM((3, columns, 8, length), f32),
             pltpu.VMEM((3, columns, 8, length), f32),
-            dma((2,)), dma((2,)), dma((3,)), dma((3,)),
+            dma((2,)), dma((2,)), dma((3,)), dma((3,)), known_shape(columns),
+            pltpu.SMEM(target.shape, jnp.int32), dma(()),
         ],
         compiler_params=pltpu.CompilerParams(
             collective_id=1, has_side_effects=True, vmem_limit_bytes=VMEM_LIMIT

time: 36.5 us -> 33.5 us (0.918); the launches traced: 35.8 us -> 34.1 us
  Pallas kernels: 34.6 us -> 32.8 us
    pallas_call x1, Pallas kernels: 16.9 us -> 15.6 us  [shards(): pl.pallas_call(functools.partial(exchange_kernel, rows, columns), out_sha...]
    pallas_call x1, Pallas kernels: 14.9 us -> 14.4 us  [shards(): pl.pallas_call(functools.partial(return_kernel, rows, columns), out_shape...]
where the time goes in v4:
time: 33.5 us; the launch traced here: 34.1 us
  Pallas kernels  32.8 us (98%)
  between operations  0.66 us (2%)
  local copies, waits for them, and re-layouts  0.6 us (2%)
    pallas_call x1, Pallas kernels, shards(): pl.pallas_call(functools.partial(exchange_kernel, rows, columns), out_sha...  15.6 us
    pallas_call x1, Pallas kernels, shards(): pl.pallas_call(functools.partial(return_kernel, rows, columns), out_shape...  14.4 us
    pallas_call x1, Pallas kernels, shards(): pl.pallas_call(functools.partial(points_kernel, depth, breadth), out_shap...  2.83 us

profile of v4, /device:TPU:0, one launch (start us, length us, event | category | flops | bytes accessed | tf_op | source)
XLA Modules:
  0.0 34.1 jit_solution(8431994010381250212)
XLA Ops:
  0.6 15.6 %shard_map.86 = (f32[3,30,48,128]{3,2,1,0:T(8,128)S(1)}, f32[3,3,8,16,128]{4,3,2,1,0:T(8,128)S(1)}, s32[8,256]{1,0:T(8,128)S(1)}) custom-call(s32[8]{0:T(128)} %bitcast.11, s32[8]{0:T(128)} %zoff_hbm.1, s32[8]{0:T(128)} %yoff_hbm.1, f32[3,16,32,128]{3,2,1,0:T(8,128)} %velocity_ref.1, f32[16,32,128]{2,1,0:T(8,128)} %viscosity_ref.1, f32[3,8,128]{2,1,0:T(8,128)} %bitcast.9, ...), custom_call_target="tpu_custom_call" | custom-call | tf_op jit(solution)/shard_map/pallas_call | solution.py:696
  16.2 2.8 %shard_map.87 = (f32[3,16,32,128]{3,2,1,0:T(8,128)}, f32[72,8,128]{2,1,0:T(8,128)S(1)}, f32[3,30,48,128]{3,2,1,0:T(8,128)S(1)}) custom-call(s32[8,256]{1,0:T(8,128)S(1)} %get-tuple-element.7.list_ref, f32[72,16,128]{2,1,0:T(8,128)S(1)} %bitcast.6, f32[3,30,48,128]{3,2,1,0:T(8,128)S(1)} %get-tuple-element.9.field_in), custom_call_target="tpu_custom_call", output_to_operand_aliasing={{2}: (2, {})} | custom-call | tf_op jit(solution)/shard_map/pallas_call | solution.py:728
  19.1 14.4 %shard_map.88 = f32[3,8,128]{2,1,0:T(8,128)S(1)} custom-call(s32[8]{0:T(128)} %bitcast.12, f32[3,3,8,8,128]{4,3,2,1,0:T(8,128)S(1)} %bitcast.7), custom_call_target="tpu_custom_call" | custom-call | tf_op jit(solution)/shard_map/pallas_call | solution.py:746
  33.5 0.6 %copy.12 = f32[8,3,128]{2,0,1:T(8,128)} copy(f32[8,3,128]{2,0,1:T(8,128)S(1)} %bitcast.8) | data formatting | bytes 24576
